TPU v7x, 128 devices: a whole 4x4x4 slice. The times are simulated.
128 devices in a mesh: adapter: 32 (over x, z, core), head: 4 (over y).
Axes of the slice: x: 4, y: 4, z: 4, core: 2. Of those that a mesh axis runs over, the one named last changes fastest.
Arguments:
- call_token_inputs: bfloat16 [1024, 32, 4096], P('adapter', None, 'head'), may hold values from -6 to 6
- routed_group_index: int32 [1024], replicated, may hold values from 0 to 31, as said below
- call_adapter_index: int32 [1024, 1], replicated, may hold values from 0 to 63
- holder_table_row: int32 [64], replicated, may hold values from 0 to 63, each once
- channel_input_weight: bfloat16 [4096, 4096], P(None, 'head'), may hold values from -0.09375 to 0.09375
- input_state_weight: bfloat16 [4096, 512], P(None, 'head'), may hold values from -0.09375 to 0.09375
- output_state_weight: bfloat16 [4096, 512], P(None, 'head'), may hold values from -0.09375 to 0.09375
- step_size_weight: bfloat16 [4096, 64], P(None, 'head'), may hold values from -0.09375 to 0.09375
- channel_input_taps: bfloat16 [4, 4096], P(None, 'head'), may hold values from -3 to 3
- input_state_taps: bfloat16 [4, 512], P(None, 'head'), may hold values from -3 to 3
- output_state_taps: bfloat16 [4, 512], P(None, 'head'), may hold values from -3 to 3
- adapter_down_weight: bfloat16 [64, 4096, 64], P('adapter', None, 'head'), may hold values from -0.09375 to 0.09375
- adapter_up_weight: bfloat16 [64, 64, 4096], P('adapter', None, 'head'), may hold values from -0.75 to 0.75
- decay_logarithm: float32 [64], P('head'), may hold values from -2.5 to 1.5
- step_size_bias: float32 [64], P('head'), may hold values from -2 to 0
- head_skip_factor: float32 [64], P('head'), may hold values from 0.5 to 1.5
Outputs:
- replies: bfloat16 [2048, 32, 4096], P('adapter', None, 'head')
Inputs may be any that keep to these rules, and one draw needn't show every extreme that they name: `routed_group_index`: among the 32 calls of one source no group is named more than 2 times, and one group is named exactly 2 times by every source. `call_adapter_index`: every adapter is named by some call. `holder_table_row`: A permutation of 0 to 63.
All inputs are finite; a program needn't handle non-finite values.
Results may differ from a plain program's by a relative error of at most 0.0035.
Values may be sent and summed in bfloat16 or wider, within the bound.
A program may use at most 192 MiB of HBM per device.

v0:
```python
import jax
import jax.numpy as jnp
from jax import lax
from jax.sharding import PartitionSpec as P

HEAD_DIM = 64
NSTATE = 128
CAP = 2
PRECISE = lax.Precision.HIGHEST


def call_ranks(group_grid):
    count = group_grid.shape[-1]
    same_group = group_grid[..., :, None] == group_grid[..., None, :]
    earlier = jnp.arange(count)[None, :] < jnp.arange(count)[:, None]
    return jnp.sum(jnp.where(same_group & earlier, 1, 0), axis=-1).astype(jnp.int32)


def causal_filter_apply(series, kernel):
    span = kernel.shape[0]
    length = series.shape[1]
    padded = jnp.pad(series, ((0, 0), (span - 1, 0), (0, 0)))
    summed = jnp.zeros(series.shape, jnp.float32)
    for offset in range(span):
        summed = (
            summed + kernel[offset].astype(jnp.float32) * padded[:, offset : offset + length, :]
        )
    return jax.nn.silu(summed)


def state_space(
    filtered_inputs, b_conv, c_conv, dt_vals, decay_logarithm, head_skip_factor, call_token_length
):
    blocks = filtered_inputs.shape[0]
    block_rows = filtered_inputs.shape[1]
    head_count = decay_logarithm.shape[0]
    group_count = b_conv.shape[2] // NSTATE
    x_heads = filtered_inputs.reshape(blocks, block_rows, head_count, HEAD_DIM)
    b_groups = b_conv.reshape(blocks, block_rows, group_count, NSTATE)
    c_groups = c_conv.reshape(blocks, block_rows, group_count, NSTATE)
    step_vals = -jnp.exp(decay_logarithm) * dt_vals
    cumulated = jnp.cumsum(jnp.moveaxis(step_vals, 2, 1), axis=2)
    row_iota = jnp.arange(block_rows)
    causal = (row_iota[:, None] // call_token_length == row_iota[None, :] // call_token_length) & (
        row_iota[None, :] <= row_iota[:, None]
    )
    segment = cumulated[:, :, :, None] - cumulated[:, :, None, :]
    decay = jnp.where(causal, jnp.exp(jnp.where(causal, segment, 0.0)), 0.0)
    routing_marks = jnp.einsum("ntgk,njgk->ngtj", c_groups, b_groups, precision=PRECISE)
    routing_marks = jnp.repeat(routing_marks, head_count // group_count, axis=1)
    mixing = routing_marks * decay * jnp.moveaxis(dt_vals, 2, 1)[:, :, None, :]
    output = (
        jnp.einsum("nhtj,njhp->nthp", mixing, x_heads, precision=PRECISE)
        + head_skip_factor[:, None] * x_heads
    )
    return output.reshape(blocks, block_rows, head_count * HEAD_DIM)


def on_device(
    call_token_inputs,
    routed_group_index,
    call_adapter_index,
    holder_table_row,
    channel_input_weight,
    input_state_weight,
    output_state_weight,
    step_size_weight,
    channel_input_taps,
    input_state_taps,
    output_state_taps,
    adapter_down_weight,
    adapter_up_weight,
    decay_logarithm,
    step_size_bias,
    head_skip_factor,
):
    sender_indices = lax.axis_size("adapter")
    my_group = lax.axis_index("adapter")
    per_source = call_token_inputs.shape[0]
    call_token_length = call_token_inputs.shape[1]
    slot_count = sender_indices * CAP
    group_grid = routed_group_index.reshape(sender_indices, per_source)
    rank_grid = call_ranks(group_grid)
    call_iota = jnp.arange(per_source, dtype=jnp.int32)
    my_groups = lax.dynamic_index_in_dim(group_grid, my_group, 0, keepdims=False)
    my_ranks = lax.dynamic_index_in_dim(rank_grid, my_group, 0, keepdims=False)
    send_slot = my_groups * CAP + my_ranks
    slot_iota = jnp.arange(slot_count, dtype=jnp.int32)
    send_match = send_slot[None, :] == slot_iota[:, None]
    send_live = jnp.any(send_match, axis=1)
    send_call = jnp.sum(jnp.where(send_match, call_iota[None, :], 0), axis=1)
    rank_iota = jnp.arange(CAP, dtype=jnp.int32)
    recv_match = (group_grid[:, None, :] == my_group) & (
        rank_grid[:, None, :] == rank_iota[None, :, None]
    )
    local_call = jnp.sum(jnp.where(recv_match, call_iota[None, None, :], 0), axis=2)
    global_call = (
        jnp.arange(sender_indices, dtype=jnp.int32)[:, None] * per_source + local_call
    ).reshape(-1)
    slot_pos = holder_table_row[call_adapter_index[global_call, 0]]
    down_weight_table, up_weight_table = (
        lax.all_gather(adapter_down_weight, "adapter", axis=0, tiled=True),
        lax.all_gather(adapter_up_weight, "adapter", axis=0, tiled=True),
    )
    slot_down_weight = jnp.take(down_weight_table, slot_pos, axis=0)
    slot_up_weight = jnp.take(up_weight_table, slot_pos, axis=0)
    features = lax.all_gather(call_token_inputs, "head", axis=2, tiled=True)
    outgoing = jnp.where(
        send_live[:, None, None],
        jnp.take(features, send_call, axis=0),
        jnp.zeros((), features.dtype),
    )
    landed_rows = lax.all_to_all(outgoing, "adapter", split_axis=0, concat_axis=0, tiled=True)
    flat_rows = landed_rows.reshape(-1, landed_rows.shape[2])
    projected_inputs = jnp.dot(flat_rows, channel_input_weight, preferred_element_type=jnp.float32)
    proj_b = jnp.dot(flat_rows, input_state_weight, preferred_element_type=jnp.float32)
    proj_c = jnp.dot(flat_rows, output_state_weight, preferred_element_type=jnp.float32)
    proj_dt = jnp.dot(flat_rows, step_size_weight, preferred_element_type=jnp.float32)
    reduced_features = jnp.einsum(
        "vxg,vgj->vxj", landed_rows, slot_down_weight, preferred_element_type=jnp.float32
    )
    local_slot_count = landed_rows.shape[0]
    reduced_every_call = lax.all_gather(
        reduced_features.astype(jnp.bfloat16), "head", axis=2, tiled=True
    )
    adapter_delta_output = jnp.einsum(
        "uce,ued->ucd", reduced_every_call, slot_up_weight, preferred_element_type=jnp.float32
    )
    filtered_inputs = causal_filter_apply(
        projected_inputs.reshape(local_slot_count, call_token_length, -1) + adapter_delta_output,
        channel_input_taps,
    )
    b_conv = causal_filter_apply(
        proj_b.reshape(local_slot_count, call_token_length, -1), input_state_taps
    )
    c_conv = causal_filter_apply(
        proj_c.reshape(local_slot_count, call_token_length, -1), output_state_taps
    )
    dt_vals = jax.nn.softplus(
        proj_dt.reshape(local_slot_count, call_token_length, -1) + step_size_bias
    )
    row_total = local_slot_count * call_token_length
    block_rows = min(128, row_total)
    blocks = row_total // block_rows

    def blocked(values):
        return values.reshape(blocks, block_rows, values.shape[2])

    output = state_space(
        blocked(filtered_inputs),
        blocked(b_conv),
        blocked(c_conv),
        blocked(dt_vals),
        decay_logarithm,
        head_skip_factor,
        call_token_length,
    )
    return output.reshape(local_slot_count, call_token_length, -1).astype(jnp.bfloat16)


def solution(mesh):
    placed = (
        P("adapter", None, "head"),
        P(),
        P(),
        P(),
        P(None, "head"),
        P(None, "head"),
        P(None, "head"),
        P(None, "head"),
        P(None, "head"),
        P(None, "head"),
        P(None, "head"),
        P("adapter", None, "head"),
        P("adapter", None, "head"),
        P("head"),
        P("head"),
        P("head"),
    )
    return jax.shard_map(
        on_device, mesh=mesh, in_specs=placed, out_specs=P("adapter", None, "head"), check_vma=False
    )
```

profile of v0, /device:TPU:44, one launch (start us, length us, event | category | flops | bytes accessed | tf_op | source)
XLA Modules:
  0.0 619.2 jit_solution(13992757347904840570)
XLA Ops:
  6.5 0.0 copy-start
  6.5 0.7 all-gather.4.cloned.1.call-update
  7.3 0.0 all-gather.6.cloned.1.call-start
  7.3 0.7 all-gather.6.cloned.1.call-update
  8.0 0.0 all-gather.8.cloned.1.call-start
  8.1 0.7 all-gather.8.cloned.1.call-update
  8.8 0.8 reshape.303
  9.5 0.8 select_reduce_fusion
  10.3 0.1 select_reduce_fusion.2
  10.4 0.1 fusion.57
  10.5 83.5 %all-gather.4.cloned.1.call-done = bf16[32,32,4096]{2,1,0:T(8,128)(2,1)} async-done(((bf16[32,32,1024]{2,1,0:T(8,128)(2,1)}), bf16[32,32,4096]{2,1,0:T(8,128)(2,1)}) %all-gather.4.cloned.1.call-update) | async-done | bytes 8388624 | tf_op jit(solution)/shard_map/all_gather | solution.py:107
  94.1 10.9 %gather_fusion = bf16[64,32,4096]{2,1,0:T(8,128)(2,1)} fusion(bf16[32,32,4096]{2,1,0:T(8,128)(2,1)} %all-gather.4.cloned.1.call-done, s32[1024]{0:T(1024)S(1)} %pad_clamp_fusion.2), kind=kCustom, calls=%fused_computation | custom fusion | bytes 33554688 | tf_op jit(solution)/shard_map/jit(_take)/gather | solution.py:110
  105.0 14.4 %select_select_fusion = bf16[64,32,4096]{2,1,0:T(8,128)(2,1)} fusion(bf16[64,32,4096]{2,1,0:T(8,128)(2,1)} %gather_fusion, pred[64]{0:T(512)(128)(4,1)S(1)} %compare_and_fusion.1, pred[64]{0:T(512)(128)(4,1)S(1)} %fusion.57), kind=kLoop, calls=%fused_computation.12 | loop fusion | flops 16777216 | bytes 33554560 | tf_op jit(solution)/shard_map/jit(_where)/select_n | solution.py:108
  119.4 0.0 copy-start.11
  119.4 0.0 copy-start.4
  119.4 7.6 %all-to-all-start = ((bf16[64,32,4096]{2,1,0:T(8,128)(2,1)}), bf16[64,32,4096]{2,1,0:T(8,128)(2,1)}, u32[]{:S(2)}, u32[]{:S(2)}) async-start(bf16[64,32,4096]{2,1,0:T(8,128)(2,1)} %select_select_fusion), calls=%async_computation | async-start | bytes 33554432 | tf_op jit(solution)/shard_map/all_to_all | solution.py:113
  127.1 0.1 select_reduce_fusion.1
  127.2 0.1 copy.31
  127.3 0.1 add.182
  127.4 0.8 gather_fusion.1
  128.2 0.8 gather_fusion.2
  129.0 0.5 exponential_negate_fusion
  129.6 0.0 copy-done.10
  129.6 0.6 bitcast_convert_fusion.7
  130.2 0.6 bitcast_convert_fusion.3
  130.8 0.7 fusion.55
  131.5 0.0 copy-done.4
  131.5 0.6 slice_convert_fusion.3
  132.1 150.0 %all-gather.6.cloned.1.call-done = bf16[64,4096,16]{1,2,0:T(8,128)(2,1)} async-done(((bf16[2,4096,16]{1,2,0:T(8,128)(2,1)}), bf16[64,4096,16]{1,2,0:T(8,128)(2,1)}) %all-gather.6.cloned.1.call-update) | async-done | bytes 8388624 | tf_op jit(solution)/shard_map/all_gather | solution.py:102
  282.0 8.9 %gather_fusion.3 = bf16[64,4096,16]{1,2,0:T(8,128)(2,1)} fusion(bf16[64,4096,16]{1,2,0:T(8,128)(2,1)} %all-gather.6.cloned.1.call-done, s32[1024]{0:T(1024)S(1)} %pad_clamp_fusion), kind=kCustom, calls=%fused_computation.3 | custom fusion | bytes 16777472 | tf_op jit(solution)/shard_map/jit(_take)/gather | solution.py:105
  291.0 105.4 %all-gather.8.cloned.1.call-done = bf16[64,64,1024]{2,1,0:T(8,128)(2,1)} async-done(((bf16[2,64,1024]{2,1,0:T(8,128)(2,1)}), bf16[64,64,1024]{2,1,0:T(8,128)(2,1)}) %all-gather.8.cloned.1.call-update) | async-done | bytes 8388624 | tf_op jit(solution)/shard_map/all_gather | solution.py:103
  396.4 8.9 %gather_fusion.4 = bf16[64,64,1024]{2,1,0:T(8,128)(2,1)} fusion(bf16[64,64,1024]{2,1,0:T(8,128)(2,1)} %all-gather.8.cloned.1.call-done, s32[1024]{0:T(1024)S(1)} %pad_clamp_fusion), kind=kCustom, calls=%fused_computation.4 | custom fusion | bytes 16777472 | tf_op jit(solution)/shard_map/jit(_take)/gather | solution.py:106
  405.3 8.6 %all-to-all-done = bf16[64,32,4096]{2,1,0:T(8,128)(2,1)} async-done(((bf16[64,32,4096]{2,1,0:T(8,128)(2,1)}), bf16[64,32,4096]{2,1,0:T(8,128)(2,1)}, u32[]{:S(2)}, u32[]{:S(2)}) %all-to-all-start) | async-done | bytes 16777248 | tf_op jit(solution)/shard_map/all_to_all | solution.py:113
  413.9 10.5 %fusion.35 = bf16[64,32,16]{1,2,0:T(8,128)(2,1)S(1)} fusion(bf16[64,32,4096]{2,1,0:T(8,128)(2,1)} %all-to-all-done, bf16[64,4096,16]{1,2,0:T(8,128)(2,1)} %gather_fusion.3, pred[64]{0:T(512)(128)(4,1)S(1)} %compare_and_fusion), kind=kOutput, calls=%fused_computation.50 | convolution fusion | flops 272662528 | bytes 25231424 | tf_op jit(solution)/shard_map/vxg,vgj->vxj/dot_general | solution.py:119
  424.4 15.9 %all_gather.14 = bf16[64,32,64]{1,2,0:T(8,128)(2,1)S(1)} all-gather(bf16[64,32,16]{1,2,0:T(8,128)(2,1)S(1)} %fusion.35), channel_id=1, replica_groups=mesh['adapter'=32,'head'=4] {'head'}, dimensions={2}, use_global_device_ids=true | all-gather | bytes 327680 | tf_op jit(solution)/shard_map/all_gather | solution.py:123
  440.3 4.8 fusion.21
  445.1 24.3 %fusion.32 = f32[64,32,1024]{2,1,0:T(8,128)} fusion(f32[64,32,1024]{2,1,0:T(8,128)S(1)} %fusion.21, bf16[64,32,4096]{2,1,0:T(8,128)(2,1)} %all-to-all-done, bf16[4096,1024]{1,0:T(8,128)(2,1)} %param.20), kind=kOutput, calls=%fused_computation.41 | convolution fusion | flops 17181966336 | bytes 41943040 | tf_op jit(solution)/shard_map/dot_general | solution.py:115
  469.4 0.0 copy-done.5
  469.4 16.3 %divide_multiply_fusion = f32[64,32,1024]{2,1,0:T(8,128)} fusion(f32[64,32,1024]{2,1,0:T(8,128)} %fusion.32, f32[1024]{0:T(1024)S(1)} %bitcast.85, f32[1024]{0:T(1024)S(1)} %bitcast.86, f32[1024]{0:T(1024)S(1)} %bitcast.84, f32[1024]{0:T(1024)S(1)} %bitcast.83), kind=kLoop, calls=%fused_computation.31 | loop fusion | flops 23068672 | bytes 16793600 | tf_op jit(solution)/shard_map/jit(silu)/mul | solution.py:28
  485.7 13.3 %reshape_reshape.2 = f32[16,128,16,64]{3,2,1,0:T(8,128)} reshape(f32[64,32,1024]{2,1,0:T(8,128)} %divide_multiply_fusion) | data formatting | bytes 16777216 | tf_op jit(solution)/shard_map/reshape;reshape | solution.py:38
  499.0 13.4 %copy.35 = f32[16,128,16,64]{1,3,2,0:T(8,128)} copy(f32[16,128,16,64]{3,2,1,0:T(8,128)} %reshape_reshape.2) | data formatting | bytes 16777216 | tf_op jit(solution)/shard_map/reshape;reshape | solution.py:38
  512.4 0.0 copy-done.12
  512.4 14.7 %compare_select_fusion = f32[64,32,16]{1,2,0:T(8,128)S(1)} fusion(bf16[64,32,4096]{2,1,0:T(8,128)(2,1)} %all-to-all-done, f32[16]{0:T(128)S(1)} %copy-done.12, bf16[4096,16]{0,1:T(8,128)(2,1)S(1)} %copy-done.3), kind=kOutput, calls=%fused_computation.42 | convolution fusion | flops 268664832 | bytes 17039424 | tf_op jit(solution)/shard_map/dot_general | solution.py:118
  527.2 0.2 copy.32
  527.3 0.2 reshape.307
  527.5 0.0 copy-done.21
  527.5 0.1 multiply_bitcast_fusion
  527.8 0.0 copy-start.22
  527.8 8.3 %fusion.52 = f32[64,32,128]{2,1,0:T(8,128)S(1)} fusion(bf16[64,32,4096]{2,1,0:T(8,128)(2,1)} %all-to-all-done, bf16[4096,128]{1,0:T(8,128)(2,1)S(1)} %copy-done), kind=kOutput, calls=%fused_computation.65 | convolution fusion | flops 2147483648 | bytes 18874368 | tf_op jit(solution)/shard_map/dot_general | solution.py:117
  536.1 0.6 divide_multiply_fusion.2
  536.7 0.0 copy-done.22
  536.7 0.0 copy-start.13
  536.7 0.0 copy-start.14
  536.7 0.0 copy-start.15
  536.8 0.0 copy-start.16
  536.8 0.0 copy-start.9
  536.8 0.0 copy-start.24
  536.8 8.2 %fusion.50 = f32[64,32,128]{2,1,0:T(8,128)S(1)} fusion(bf16[64,32,4096]{2,1,0:T(8,128)(2,1)} %all-to-all-done, bf16[4096,128]{1,0:T(8,128)(2,1)S(1)} %copy-done.22), kind=kOutput, calls=%fused_computation.63 | convolution fusion | flops 2147483648 | bytes 18874368 | tf_op jit(solution)/shard_map/dot_general | solution.py:116
  545.0 0.6 divide_multiply_fusion.1
  545.6 2.3 fusion.67
  547.9 4.5 reduce_window_sum.11
  552.5 38.2 %fusion.13 = bf16[16,128,16,64]{1,3,2,0:T(8,128)(2,1)} fusion(f32[16,128,16,64]{1,3,2,0:T(8,128)} %copy.35, f32[16]{0:T(128)S(1)} %copy-done.24, f32[16,16,128]{2,1,0:T(8,128)S(1)} %copy.34, f32[16,16,128]{2,1,0:T(8,128)S(1)} %reduce_window_sum.11, f32[16,128,128]{2,1,0:T(8,128)S(1)} %fusion.67, pred[128,128]{1,0:T(8,128)(4,1)S(1)} %copy-done.9), kind=kOutput, calls=%fused_computation.23 | convolution fusion | flops 3248488448 | bytes 13910080 | tf_op jit(solution)/shard_map/nhtj,njhp->nthp/dot_general | solution.py:53
  590.7 10.1 %copy.37 = bf16[16,128,16,64]{3,2,1,0:T(8,128)(2,1)} copy(bf16[16,128,16,64]{1,3,2,0:T(8,128)(2,1)} %fusion.13) | data formatting | bytes 8388608 | tf_op jit(solution)/shard_map/convert_element_type | solution.py:158
  600.8 11.9 %convert_element_type.160 = bf16[64,32,1024]{2,1,0:T(8,128)(2,1)} reshape(bf16[16,128,16,64]{3,2,1,0:T(8,128)(2,1)} %copy.37) | data formatting | bytes 8388608 | tf_op jit(solution)/shard_map/convert_element_type | solution.py:158
  (52 shorter events, 0.3 us)
Async XLA Ops:
  6.5 521.2 %copy-start = (bf16[4096,128]{1,0:T(8,128)(2,1)S(1)}, bf16[4096,128]{1,0:T(8,128)(2,1)}, u32[]{:S(2)}) copy-start(bf16[4096,128]{1,0:T(8,128)(2,1)} %param.22) | copy-start | bytes 3145732
  6.5 87.5 %all-gather.4.cloned.1.call-start = ((), (), s32[]{:S(2)}) async-start(), calls=%async_computation.1 | async-start | bytes 10485760 | tf_op jit(solution)/shard_map/all_gather | solution.py:107
  7.3 274.8 %all-gather.6.cloned.1.call-start = ((), (), s32[]{:S(2)}) async-start(), calls=%async_computation.2 | async-start | bytes 8650752 | tf_op jit(solution)/shard_map/all_gather | solution.py:102
  8.0 388.4 %all-gather.8.cloned.1.call-start = ((), (), s32[]{:S(2)}) async-start(), calls=%async_computation.3 | async-start | bytes 8650752 | tf_op jit(solution)/shard_map/all_gather | solution.py:103
  119.4 8.0 %copy-start.2 = (s32[1024,1]{0,1:T(1,128)S(1)}, s32[1024,1]{0,1:T(1,128)}, u32[]{:S(2)}) copy-start(s32[1024,1]{0,1:T(1,128)} %param.18) | copy-start | bytes 12292
  119.4 8.8 %copy-start.1 = (s32[64]{0:T(128)S(1)}, s32[64]{0:T(128)}, u32[]{:S(2)}) copy-start(s32[64]{0:T(128)} %param.19) | copy-start | bytes 772
  119.4 9.7 %copy-start.23 = (f32[16]{0:T(128)S(1)}, f32[16]{0:T(128)}, u32[]{:S(2)}) copy-start(f32[16]{0:T(128)} %param.29) | copy-start | bytes 196
  119.4 10.2 %copy-start.10 = (bf16[4,128]{1,0:T(4,128)(2,1)S(1)}, bf16[4,128]{1,0:T(4,128)(2,1)}, u32[]{:S(2)}) copy-start(bf16[4,128]{1,0:T(4,128)(2,1)} %param.26) | copy-start | bytes 3076
  119.4 10.8 %copy-start.11 = (bf16[4,128]{1,0:T(4,128)(2,1)S(1)}, bf16[4,128]{1,0:T(4,128)(2,1)}, u32[]{:S(2)}) copy-start(bf16[4,128]{1,0:T(4,128)(2,1)} %param.25) | copy-start | bytes 3076
  119.4 12.1 %copy-start.4 = (bf16[4,1024]{1,0:T(4,128)(2,1)S(1)}, bf16[4,1024]{1,0:T(4,128)(2,1)}, u32[]{:S(2)}) copy-start(bf16[4,1024]{1,0:T(4,128)(2,1)} %param.24) | copy-start | bytes 24580
  119.4 294.5 %all-to-all-start = ((bf16[64,32,4096]{2,1,0:T(8,128)(2,1)}), bf16[64,32,4096]{2,1,0:T(8,128)(2,1)}, u32[]{:S(2)}, u32[]{:S(2)}) async-start(bf16[64,32,4096]{2,1,0:T(8,128)(2,1)} %select_select_fusion), calls=%async_computation | async-start | bytes 33554432 | tf_op jit(solution)/shard_map/all_to_all | solution.py:113
  445.1 24.3 %copy-start.5 = (f32[1,1024]{1,0:T(1,128)S(1)}, f32[1,1024]{1,0:T(1,128)}, u32[]{:S(2)}) copy-start(f32[1,1024]{1,0:T(1,128)} %get-tuple-element.5) | copy-start | bytes 12292
  445.1 24.3 %copy-start.6 = (f32[1,1024]{1,0:T(1,128)S(1)}, f32[1,1024]{1,0:T(1,128)}, u32[]{:S(2)}) copy-start(f32[1,1024]{1,0:T(1,128)} %get-tuple-element.6) | copy-start | bytes 12292
  445.1 24.3 %copy-start.7 = (f32[1,1024]{1,0:T(1,128)S(1)}, f32[1,1024]{1,0:T(1,128)}, u32[]{:S(2)}) copy-start(f32[1,1024]{1,0:T(1,128)} %get-tuple-element.7) | copy-start | bytes 12292
  445.1 24.3 %copy-start.8 = (f32[1,1024]{1,0:T(1,128)S(1)}, f32[1,1024]{1,0:T(1,128)}, u32[]{:S(2)}) copy-start(f32[1,1024]{1,0:T(1,128)} %get-tuple-element.8) | copy-start | bytes 12292
  499.0 13.4 %copy-start.3 = (bf16[4096,16]{0,1:T(8,128)(2,1)S(1)}, bf16[4096,16]{0,1:T(8,128)(2,1)}, u32[]{:S(2)}) copy-start(bf16[4096,16]{0,1:T(8,128)(2,1)} %param.23) | copy-start | bytes 393220
  499.0 13.4 %copy-start.12 = (f32[16]{0:T(128)S(1)}, f32[16]{0:T(128)}, u32[]{:S(2)}) copy-start(f32[16]{0:T(128)} %param.30) | copy-start | bytes 196
  512.4 15.1 %copy-start.21 = (f32[16]{0:T(128)S(1)}, f32[16]{0:T(128)}, u32[]{:S(2)}) copy-start(f32[16]{0:T(128)} %exponential_negate_fusion) | copy-start | bytes 196
  527.7 8.3 %copy-start.17 = (f32[128]{0:T(128)S(1)}, f32[128]{0:T(128)}, u32[]{:S(2)}) copy-start(f32[128]{0:T(128)} %get-tuple-element.13) | copy-start | bytes 1540
  527.7 8.3 %copy-start.18 = (f32[128]{0:T(128)S(1)}, f32[128]{0:T(128)}, u32[]{:S(2)}) copy-start(f32[128]{0:T(128)} %get-tuple-element.14) | copy-start | bytes 1540
  527.7 8.3 %copy-start.19 = (f32[128]{0:T(128)S(1)}, f32[128]{0:T(128)}, u32[]{:S(2)}) copy-start(f32[128]{0:T(128)} %get-tuple-element.15) | copy-start | bytes 1540
  527.8 8.3 %copy-start.20 = (f32[128]{0:T(128)S(1)}, f32[128]{0:T(128)}, u32[]{:S(2)}) copy-start(f32[128]{0:T(128)} %get-tuple-element.16) | copy-start | bytes 1540
  527.8 8.9 %copy-start.22 = (bf16[4096,128]{1,0:T(8,128)(2,1)S(1)}, bf16[4096,128]{1,0:T(8,128)(2,1)}, u32[]{:S(2)}) copy-start(bf16[4096,128]{1,0:T(8,128)(2,1)} %param.21) | copy-start | bytes 3145732
  536.7 8.3 %copy-start.13 = (f32[128]{0:T(128)S(1)}, f32[128]{0:T(128)}, u32[]{:S(2)}) copy-start(f32[128]{0:T(128)} %get-tuple-element.9) | copy-start | bytes 1540
  536.7 8.3 %copy-start.14 = (f32[128]{0:T(128)S(1)}, f32[128]{0:T(128)}, u32[]{:S(2)}) copy-start(f32[128]{0:T(128)} %get-tuple-element.10) | copy-start | bytes 1540
  536.7 8.3 %copy-start.15 = (f32[128]{0:T(128)S(1)}, f32[128]{0:T(128)}, u32[]{:S(2)}) copy-start(f32[128]{0:T(128)} %get-tuple-element.11) | copy-start | bytes 1540
  536.8 8.3 %copy-start.16 = (f32[128]{0:T(128)S(1)}, f32[128]{0:T(128)}, u32[]{:S(2)}) copy-start(f32[128]{0:T(128)} %get-tuple-element.12) | copy-start | bytes 1540
  536.8 15.7 %copy-start.9 = (pred[128,128]{1,0:T(8,128)(4,1)S(1)}, pred[128,128]{1,0:T(8,128)(4,1)}, u32[]{:S(2)}) copy-start(pred[128,128]{1,0:T(8,128)(4,1)} %fusion.55) | copy-start | bytes 49156
  536.8 15.7 %copy-start.24 = (f32[16]{0:T(128)S(1)}, f32[16]{0:T(128)}, u32[]{:S(2)}) copy-start(f32[16]{0:T(128)} %param.31) | copy-start | bytes 196
Sparse Core Ops, SparseCore 0:
  9.0 84.9 all-gather.3
  96.3 185.6 all-gather.5
  284.3 112.0 all-gather.7
where the time goes:
time: 621 us; the launch traced here: 619 us
  waiting for transfers between devices  350 us (56%)
  matrix products  111 us (18%)
  local copies, waits for them, and re-layouts  80.4 us (13%)
  other arithmetic  40.8 us (7%)
  blocking collectives  15.9 us (3%)
  between operations  13.6 us (2%)
  starting transfers between devices  7.7 us (1%)
    all_gather x1, waiting for transfers between devices, on_device(): lax.all_gather(adapter_down_weight, 'adapter', axis=0, tiled=True)  150 us
    all_gather x1, waiting for transfers between devices, on_device(): lax.all_gather(adapter_up_weight, 'adapter', axis=0, tiled=True)  105 us
    all_gather x1, waiting for transfers between devices, on_device(): features = lax.all_gather(call_token_inputs, 'head', axis=2, tiled=True)  83.5 us
    dot_general x1, matrix products, state_space(): jnp.einsum('nhtj,njhp->nthp', mixing, x_heads, precision=PRECISE)  38.2 us
    another operation x2, local copies, waits for them, and re-layouts, state_space(): x_heads = filtered_inputs.reshape(blocks, block_rows, head_count, HEAD_DIM)  26.7 us
    dot_general x1, matrix products, on_device(): jnp.dot(flat_rows, channel_input_weight, preferred_element_type=jnp.float32)  24.3 us
    convert_element_type x2, local copies, waits for them, and re-layouts, on_device(): output.reshape(local_slot_count, call_token_length, -1).astype(jnp.bfloat16)  21.9 us
    mul x3, other arithmetic, causal_filter_apply(): return jax.nn.silu(summed)  17.5 us
  transfers between devices with their start and end apart: 4, of which 4 were waited for; matrix products, arithmetic and copies ran while one was open for 8% of the time, Pallas kernels for 0%

commit v1 on v0

--- a/solution.py
+++ b/solution.py
@@ -2,11 +2,27 @@
 import jax.numpy as jnp
 from jax import lax
 from jax.sharding import PartitionSpec as P
+from jax.lax import axis_index, axis_size, ppermute
 
 HEAD_DIM = 64
 NSTATE = 128
 CAP = 2
 PRECISE = lax.Precision.HIGHEST
+
+
+def rest_skins_up(vals, dim_at):
+    by_rank = [vals]
+    ix = 0
+    chips = axis_size("head")
+    while ix < chips - 1:
+        by_rank.append(
+            ppermute(
+                by_rank[-1], axis_name="head", perm=[(rr, (rr + 1) % chips) for rr in range(chips)]
+            )
+        )
+        ix = ix + 1
+    w1 = jnp.concatenate(by_rank[::-1], axis=dim_at)
+    return jnp.roll(w1, shift=(axis_index("head") + 1) * vals.shape[dim_at], axis=dim_at)
 
 
 def call_ranks(group_grid):
@@ -104,7 +120,7 @@
     )
     slot_down_weight = jnp.take(down_weight_table, slot_pos, axis=0)
     slot_up_weight = jnp.take(up_weight_table, slot_pos, axis=0)
-    features = lax.all_gather(call_token_inputs, "head", axis=2, tiled=True)
+    features = rest_skins_up(call_token_inputs, dim_at=2)
     outgoing = jnp.where(
         send_live[:, None, None],
         jnp.take(features, send_call, axis=0),

time: 621 us -> 696 us (1.12); the launches traced: 619 us -> 683 us
  waiting for transfers between devices: 350 us -> 382 us
  local copies, waits for them, and re-layouts: 80.4 us -> 109 us
    all_to_all x1, waiting for transfers between devices: 8.6 us -> 247 us  [on_device(): lax.all_to_all(outgoing, 'adapter', split_axis=0, concat_axis=0, tiled=True)]
    all_gather x1, waiting for transfers between devices: 150 us -> 0.01 us  [on_device(): lax.all_gather(adapter_down_weight, 'adapter', axis=0, tiled=True)]
    ppermute x0 -> x3, waiting for transfers between devices: none -> 135 us  [rest_skins_up(): ppermute(by_rank[-1], axis_name='head', perm=[(rr, (rr + 1) % chips) for...]
    all_gather x1, waiting for transfers between devices: 105 us -> 0.01 us  [on_device(): lax.all_gather(adapter_up_weight, 'adapter', axis=0, tiled=True)]
    all_gather x1 -> x0, waiting for transfers between devices: 83.5 us -> none  [on_device(): features = lax.all_gather(call_token_inputs, 'head', axis=2, tiled=True)]
    unnamed x50 -> x67, local copies, waits for them, and re-layouts: 0.11 us -> 18.9 us
    dynamic_slice x0 -> x1, local copies, waits for them, and re-layouts: none -> 7.74 us  [rest_skins_up(): jnp.roll(w1, shift=(axis_index('head') + 1) * vals.shape[dim_at], axis=di...]
  transfers between devices with their start and end apart: 4 -> 6, of which waited for: 4 -> 4; matrix products, arithmetic and copies ran while one was open for 8% -> 11% of each run, Pallas kernels for 0% -> 0%
where the time goes in v1:
time: 696 us; the launch traced here: 683 us
  waiting for transfers between devices  382 us (55%)
  local copies, waits for them, and re-layouts  109 us (16%)
  matrix products  108 us (16%)
  other arithmetic  41 us (6%)
  blocking collectives  14.8 us (2%)
  between operations  14.3 us (2%)
  starting transfers between devices  13.2 us (2%)
    all_to_all x1, waiting for transfers between devices, on_device(): lax.all_to_all(outgoing, 'adapter', split_axis=0, concat_axis=0, tiled=True)  247 us
    ppermute x3, waiting for transfers between devices, rest_skins_up(): ppermute(by_rank[-1], axis_name='head', perm=[(rr, (rr + 1) % chips) for...  135 us
    dot_general x1, matrix products, state_space(): jnp.einsum('nhtj,njhp->nthp', mixing, x_heads, precision=PRECISE)  35.1 us
    another operation x2, local copies, waits for them, and re-layouts, state_space(): x_heads = filtered_inputs.reshape(blocks, block_rows, head_count, HEAD_DIM)  26.7 us
    dot_general x1, matrix products, on_device(): jnp.dot(flat_rows, channel_input_weight, preferred_element_type=jnp.float32)  24.3 us
    convert_element_type x2, local copies, waits for them, and re-layouts, on_device(): output.reshape(local_slot_count, call_token_length, -1).astype(jnp.bfloat16)  22 us
    unnamed x67, local copies, waits for them, and re-layouts  18.9 us
    mul x3, other arithmetic, causal_filter_apply(): return jax.nn.silu(summed)  17.6 us
  transfers between devices with their start and end apart: 6, of which 4 were waited for; matrix products, arithmetic and copies ran while one was open for 11% of the time, Pallas kernels for 0%

profile of v1, /device:TPU:44, one launch (start us, length us, event | category | flops | bytes accessed | tf_op | source)
XLA Modules:
  0.0 682.6 jit_solution(10476989206198097374)
XLA Ops:
  6.5 0.7 all-gather.3.cloned.1.call-update
  7.3 0.0 all-gather.5.cloned.1.call-start
  7.3 1.6 collective-permute-start
  9.0 46.0 %collective-permute-done = bf16[32,32,1024]{2,1,0:T(8,128)(2,1)S(1)} collective-permute-done((bf16[32,32,1024]{2,1,0:T(8,128)(2,1)}, bf16[32,32,1024]{2,1,0:T(8,128)(2,1)S(1)}, u32[]{:S(2)}, u32[]{:S(2)}) %collective-permute-start) | collective-permute-done | bytes 2097184 | tf_op jit(solution)/shard_map/ppermute | solution.py:19
  55.0 1.3 copy-done.4
  56.3 1.6 collective-permute-start.1
  57.9 45.1 %collective-permute-done.1 = bf16[32,32,1024]{2,1,0:T(8,128)(2,1)} collective-permute-done((bf16[32,32,1024]{2,1,0:T(8,128)(2,1)S(1)}, bf16[32,32,1024]{2,1,0:T(8,128)(2,1)}, u32[]{:S(2)}, u32[]{:S(2)}) %collective-permute-start.1) | collective-permute-done | bytes 2097184 | tf_op jit(solution)/shard_map/ppermute | solution.py:19
  103.0 1.6 collective-permute-start.2
  104.6 0.0 all-gather.5.cloned.1.call-update
  104.6 0.8 reshape.303
  105.4 0.8 select_reduce_fusion
  106.2 0.1 select_reduce_fusion.2
  106.3 0.1 fusion.57
  106.4 43.7 %collective-permute-done.2 = bf16[32,32,1024]{2,1,0:T(8,128)(2,1)} collective-permute-done((bf16[32,32,1024]{2,1,0:T(8,128)(2,1)}, bf16[32,32,1024]{2,1,0:T(8,128)(2,1)}, u32[]{:S(2)}, u32[]{:S(2)}) %collective-permute-start.2) | collective-permute-done | bytes 2097184 | tf_op jit(solution)/shard_map/ppermute | solution.py:19
  150.1 3.3 constant_dynamic-update-slice_fusion.7
  153.4 3.3 constant_dynamic-update-slice_fusion.6
  156.7 1.5 constant_dynamic-update-slice_fusion.5
  158.2 1.5 constant_dynamic-update-slice_fusion.4
  159.7 3.2 constant_dynamic-update-slice_fusion.3
  162.9 3.2 constant_dynamic-update-slice_fusion.2
  166.1 1.5 constant_dynamic-update-slice_fusion.1
  167.6 1.6 constant_dynamic-update-slice_fusion
  169.2 7.7 %constant_dynamic-slice_fusion = bf16[32,32,4096]{2,1,0:T(8,128)(2,1)} fusion(bf16[32,32,8192]{2,1,0:T(8,128)(2,1)} %constant_dynamic-update-slice_fusion, s32[]{:T(128)S(6)} %select_n.135), kind=kLoop, calls=%fused_computation.109 | loop fusion | bytes 16777220 | tf_op jit(solution)/shard_map/jit(_roll_dynamic)/dynamic_slice | solution.py:25
  176.9 10.9 %gather_fusion = bf16[64,32,4096]{2,1,0:T(8,128)(2,1)} fusion(bf16[32,32,4096]{2,1,0:T(8,128)(2,1)} %constant_dynamic-slice_fusion, s32[1024]{0:T(1024)S(1)} %pad_clamp_fusion.2), kind=kCustom, calls=%fused_computation | custom fusion | bytes 33554688 | tf_op jit(solution)/shard_map/jit(_take)/gather | solution.py:126
  187.8 14.3 %select_select_fusion = bf16[64,32,4096]{2,1,0:T(8,128)(2,1)} fusion(bf16[64,32,4096]{2,1,0:T(8,128)(2,1)} %gather_fusion, pred[64]{0:T(512)(128)(4,1)S(1)} %compare_and_fusion.1, pred[64]{0:T(512)(128)(4,1)S(1)} %fusion.57), kind=kLoop, calls=%fused_computation.12 | loop fusion | flops 16777216 | bytes 33554560 | tf_op jit(solution)/shard_map/jit(_where)/select_n | solution.py:124
  202.2 0.0 copy-start.14
  202.2 0.0 copy-start.7
  202.2 8.4 %all-to-all-start = ((bf16[64,32,4096]{2,1,0:T(8,128)(2,1)}), bf16[64,32,4096]{2,1,0:T(8,128)(2,1)}, u32[]{:S(2)}, u32[]{:S(2)}) async-start(bf16[64,32,4096]{2,1,0:T(8,128)(2,1)} %select_select_fusion), calls=%async_computation | async-start | bytes 33554432 | tf_op jit(solution)/shard_map/all_to_all | solution.py:129
  210.6 0.1 select_reduce_fusion.1
  210.7 0.1 copy.31
  210.8 0.1 add.198
  210.9 0.8 gather_fusion.1
  211.7 0.8 gather_fusion.2
  212.6 0.6 exponential_negate_fusion
  213.2 0.6 bitcast_convert_fusion.7
  213.7 0.6 bitcast_convert_fusion.3
  214.3 0.7 fusion.55
  215.0 0.6 slice_convert_fusion.3
  215.7 8.9 %gather_fusion.3 = bf16[64,4096,16]{1,2,0:T(8,128)(2,1)} fusion(bf16[64,4096,16]{1,2,0:T(8,128)(2,1)} %all-gather.3.cloned.1.call-done, s32[1024]{0:T(1024)S(1)} %pad_clamp_fusion), kind=kCustom, calls=%fused_computation.3 | custom fusion | bytes 16777472 | tf_op jit(solution)/shard_map/jit(_take)/gather | solution.py:121
  224.6 8.9 %gather_fusion.4 = bf16[64,64,1024]{2,1,0:T(8,128)(2,1)} fusion(bf16[64,64,1024]{2,1,0:T(8,128)(2,1)} %all-gather.5.cloned.1.call-done, s32[1024]{0:T(1024)S(1)} %pad_clamp_fusion), kind=kCustom, calls=%fused_computation.4 | custom fusion | bytes 16777472 | tf_op jit(solution)/shard_map/jit(_take)/gather | solution.py:122
  233.5 246.8 %all-to-all-done = bf16[64,32,4096]{2,1,0:T(8,128)(2,1)} async-done(((bf16[64,32,4096]{2,1,0:T(8,128)(2,1)}), bf16[64,32,4096]{2,1,0:T(8,128)(2,1)}, u32[]{:S(2)}, u32[]{:S(2)}) %all-to-all-start) | async-done | bytes 16777248 | tf_op jit(solution)/shard_map/all_to_all | solution.py:129
  480.3 10.6 %fusion.35 = bf16[64,32,16]{1,2,0:T(8,128)(2,1)S(1)} fusion(bf16[64,32,4096]{2,1,0:T(8,128)(2,1)} %all-to-all-done, bf16[64,4096,16]{1,2,0:T(8,128)(2,1)} %gather_fusion.3, pred[64]{0:T(512)(128)(4,1)S(1)} %compare_and_fusion), kind=kOutput, calls=%fused_computation.50 | convolution fusion | flops 272662528 | bytes 25231424 | tf_op jit(solution)/shard_map/vxg,vgj->vxj/dot_general | solution.py:135
  490.9 14.8 %all_gather.10 = bf16[64,32,64]{1,2,0:T(8,128)(2,1)S(1)} all-gather(bf16[64,32,16]{1,2,0:T(8,128)(2,1)S(1)} %fusion.35), channel_id=1, replica_groups=mesh['adapter'=32,'head'=4] {'head'}, dimensions={2}, use_global_device_ids=true | all-gather | bytes 327680 | tf_op jit(solution)/shard_map/all_gather | solution.py:139
  505.7 4.8 fusion.21
  510.5 24.3 %fusion.32 = f32[64,32,1024]{2,1,0:T(8,128)} fusion(f32[64,32,1024]{2,1,0:T(8,128)S(1)} %fusion.21, bf16[64,32,4096]{2,1,0:T(8,128)(2,1)} %all-to-all-done, bf16[4096,1024]{1,0:T(8,128)(2,1)} %param.20), kind=kOutput, calls=%fused_computation.41 | convolution fusion | flops 17181966336 | bytes 41943040 | tf_op jit(solution)/shard_map/dot_general | solution.py:131
  534.8 16.3 %divide_multiply_fusion = f32[64,32,1024]{2,1,0:T(8,128)} fusion(f32[64,32,1024]{2,1,0:T(8,128)} %fusion.32, f32[1024]{0:T(1024)S(1)} %bitcast.87, f32[1024]{0:T(1024)S(1)} %bitcast.88, f32[1024]{0:T(1024)S(1)} %bitcast.86, f32[1024]{0:T(1024)S(1)} %bitcast.85), kind=kLoop, calls=%fused_computation.31 | loop fusion | flops 23068672 | bytes 16793600 | tf_op jit(solution)/shard_map/jit(silu)/mul | solution.py:44
  551.1 13.3 %reshape_reshape.2 = f32[16,128,16,64]{3,2,1,0:T(8,128)} reshape(f32[64,32,1024]{2,1,0:T(8,128)} %divide_multiply_fusion) | data formatting | bytes 16777216 | tf_op jit(solution)/shard_map/reshape;reshape | solution.py:54
  564.4 13.4 %copy.35 = f32[16,128,16,64]{1,3,2,0:T(8,128)} copy(f32[16,128,16,64]{3,2,1,0:T(8,128)} %reshape_reshape.2) | data formatting | bytes 16777216 | tf_op jit(solution)/shard_map/reshape;reshape | solution.py:54
  577.8 14.5 %compare_select_fusion = f32[64,32,16]{1,2,0:T(8,128)S(1)} fusion(bf16[64,32,4096]{2,1,0:T(8,128)(2,1)} %all-to-all-done, f32[16]{0:T(128)S(1)} %copy-done.15, bf16[4096,16]{0,1:T(8,128)(2,1)S(1)} %copy-done.6), kind=kOutput, calls=%fused_computation.42 | convolution fusion | flops 268664832 | bytes 17039424 | tf_op jit(solution)/shard_map/dot_general | solution.py:134
  592.3 0.2 copy.32
  592.5 0.2 reshape.307
  592.7 0.1 multiply_bitcast_fusion
  592.9 4.8 reduce_window_sum.11
  597.7 0.0 copy-start.25
  597.7 8.3 %fusion.52 = f32[64,32,128]{2,1,0:T(8,128)S(1)} fusion(bf16[64,32,4096]{2,1,0:T(8,128)(2,1)} %all-to-all-done, bf16[4096,128]{1,0:T(8,128)(2,1)S(1)} %copy-done), kind=kOutput, calls=%fused_computation.65 | convolution fusion | flops 2147483648 | bytes 18874368 | tf_op jit(solution)/shard_map/dot_general | solution.py:133
  606.0 0.6 divide_multiply_fusion.2
  606.7 0.0 copy-start.12
  606.7 0.0 copy-start.27
  606.7 8.5 %fusion.50 = f32[64,32,128]{2,1,0:T(8,128)S(1)} fusion(bf16[64,32,4096]{2,1,0:T(8,128)(2,1)} %all-to-all-done, bf16[4096,128]{1,0:T(8,128)(2,1)S(1)} %copy-done.25), kind=kOutput, calls=%fused_computation.63 | convolution fusion | flops 2147483648 | bytes 18874368 | tf_op jit(solution)/shard_map/dot_general | solution.py:132
  615.3 0.6 divide_multiply_fusion.1
  616.0 2.3 fusion.70
  618.3 35.1 %fusion.13 = bf16[16,128,16,64]{1,3,2,0:T(8,128)(2,1)} fusion(f32[16,128,16,64]{1,3,2,0:T(8,128)S(1)} %bitcast.81, f32[16]{0:T(128)S(1)} %copy-done.27, f32[16,16,128]{2,1,0:T(8,128)S(1)} %copy.34, f32[16,16,128]{2,1,0:T(8,128)S(1)} %reduce_window_sum.11, f32[16,128,128]{2,1,0:T(8,128)S(1)} %fusion.70, pred[128,128]{1,0:T(8,128)(4,1)S(1)} %copy-done.12), kind=kOutput, calls=%fused_computation.23 | convolution fusion | flops 3248488448 | bytes 13910080 | tf_op jit(solution)/shard_map/nhtj,njhp->nthp/dot_general | solution.py:69
  653.4 10.1 %copy.37 = bf16[16,128,16,64]{3,2,1,0:T(8,128)(2,1)} copy(bf16[16,128,16,64]{1,3,2,0:T(8,128)(2,1)} %fusion.13) | data formatting | bytes 8388608 | tf_op jit(solution)/shard_map/convert_element_type | solution.py:174
  663.5 11.9 %convert_element_type.160 = bf16[64,32,1024]{2,1,0:T(8,128)(2,1)} reshape(bf16[16,128,16,64]{3,2,1,0:T(8,128)(2,1)} %copy.37) | data formatting | bytes 8388608 | tf_op jit(solution)/shard_map/convert_element_type | solution.py:174
  (75 shorter events, 0.3 us)
Async XLA Ops:
  6.5 591.1 %copy-start = (bf16[4096,128]{1,0:T(8,128)(2,1)S(1)}, bf16[4096,128]{1,0:T(8,128)(2,1)}, u32[]{:S(2)}) copy-start(bf16[4096,128]{1,0:T(8,128)(2,1)} %param.22) | copy-start | bytes 3145732
  6.5 151.7 %copy-start.3 = (bf16[32,32,1024]{2,1,0:T(8,128)(2,1)S(1)}, bf16[32,32,1024]{2,1,0:T(8,128)(2,1)}, u32[]{:S(2)}) copy-start(bf16[32,32,1024]{2,1,0:T(8,128)(2,1)} %param.16) | copy-start | bytes 6291460
  6.5 209.1 %all-gather.3.cloned.1.call-start = ((), (), s32[]{:S(2)}) async-start(), calls=%async_computation.1 | async-start | bytes 8650752 | tf_op jit(solution)/shard_map/all_gather | solution.py:118
  7.3 217.3 %all-gather.5.cloned.1.call-start = ((), (), s32[]{:S(2)}) async-start(), calls=%async_computation.2 | async-start | bytes 8650752 | tf_op jit(solution)/shard_map/all_gather | solution.py:119
  7.3 47.6 %collective-permute-start = (bf16[32,32,1024]{2,1,0:T(8,128)(2,1)}, bf16[32,32,1024]{2,1,0:T(8,128)(2,1)S(1)}, u32[]{:S(2)}, u32[]{:S(2)}) collective-permute-start(bf16[32,32,1024]{2,1,0:T(8,128)(2,1)} %param.16), channel_id=1, source_target_pairs={{0,1},{1,2},{2,3},{3,0},{4,5},{5,6},{6,7},{7,4},{8,9},{9,10},{10,1... | collective-permute-start | bytes 6291464 | tf_op jit(solution)/shard_map/ppermute | solution.py:19
  55.0 1.3 copy-start.4
  56.3 46.7 %collective-permute-start.1 = (bf16[32,32,1024]{2,1,0:T(8,128)(2,1)S(1)}, bf16[32,32,1024]{2,1,0:T(8,128)(2,1)}, u32[]{:S(2)}, u32[]{:S(2)}) collective-permute-start(bf16[32,32,1024]{2,1,0:T(8,128)(2,1)S(1)} %collective-permute-done), channel_id=1, source_target_pairs={{0,1},{1,2},{2,3},{3,0},{4,5},{5,6},{6,7},{7,4},{8,9},{9,10},{10,1... | collective-permute-start | bytes 6291464 | tf_op jit(solution)/shard_map/ppermute | solution.py:19
  103.0 47.1 %collective-permute-start.2 = (bf16[32,32,1024]{2,1,0:T(8,128)(2,1)}, bf16[32,32,1024]{2,1,0:T(8,128)(2,1)}, u32[]{:S(2)}, u32[]{:S(2)}) collective-permute-start(bf16[32,32,1024]{2,1,0:T(8,128)(2,1)} %collective-permute-done.1), channel_id=1, source_target_pairs={{0,1},{1,2},{2,3},{3,0},{4,5},{5,6},{6,7},{7,4},{8,9},{9,10},{10,1... | collective-permute-start | bytes 6291464 | tf_op jit(solution)/shard_map/ppermute | solution.py:19
  105.4 51.4 %copy-start.5 = (bf16[32,32,1024]{2,1,0:T(8,128)(2,1)S(1)}, bf16[32,32,1024]{2,1,0:T(8,128)(2,1)}, u32[]{:S(2)}) copy-start(bf16[32,32,1024]{2,1,0:T(8,128)(2,1)} %copy-done.4) | copy-start | bytes 6291460
  202.2 8.8 %copy-start.2 = (s32[1024,1]{0,1:T(1,128)S(1)}, s32[1024,1]{0,1:T(1,128)}, u32[]{:S(2)}) copy-start(s32[1024,1]{0,1:T(1,128)} %param.18) | copy-start | bytes 12292
  202.2 9.6 %copy-start.1 = (s32[64]{0:T(128)S(1)}, s32[64]{0:T(128)}, u32[]{:S(2)}) copy-start(s32[64]{0:T(128)} %param.19) | copy-start | bytes 772
  202.2 10.4 %copy-start.26 = (f32[16]{0:T(128)S(1)}, f32[16]{0:T(128)}, u32[]{:S(2)}) copy-start(f32[16]{0:T(128)} %param.29) | copy-start | bytes 196
  202.2 11.0 %copy-start.13 = (bf16[4,128]{1,0:T(4,128)(2,1)S(1)}, bf16[4,128]{1,0:T(4,128)(2,1)}, u32[]{:S(2)}) copy-start(bf16[4,128]{1,0:T(4,128)(2,1)} %param.26) | copy-start | bytes 3076
  202.2 11.6 %copy-start.14 = (bf16[4,128]{1,0:T(4,128)(2,1)S(1)}, bf16[4,128]{1,0:T(4,128)(2,1)}, u32[]{:S(2)}) copy-start(bf16[4,128]{1,0:T(4,128)(2,1)} %param.25) | copy-start | bytes 3076
  202.2 12.8 %copy-start.7 = (bf16[4,1024]{1,0:T(4,128)(2,1)S(1)}, bf16[4,1024]{1,0:T(4,128)(2,1)}, u32[]{:S(2)}) copy-start(bf16[4,1024]{1,0:T(4,128)(2,1)} %param.24) | copy-start | bytes 24580
  202.2 278.1 %all-to-all-start = ((bf16[64,32,4096]{2,1,0:T(8,128)(2,1)}), bf16[64,32,4096]{2,1,0:T(8,128)(2,1)}, u32[]{:S(2)}, u32[]{:S(2)}) async-start(bf16[64,32,4096]{2,1,0:T(8,128)(2,1)} %select_select_fusion), calls=%async_computation | async-start | bytes 33554432 | tf_op jit(solution)/shard_map/all_to_all | solution.py:129
  510.4 24.3 %copy-start.8 = (f32[1,1024]{1,0:T(1,128)S(1)}, f32[1,1024]{1,0:T(1,128)}, u32[]{:S(2)}) copy-start(f32[1,1024]{1,0:T(1,128)} %get-tuple-element.5) | copy-start | bytes 12292
  510.5 24.3 %copy-start.9 = (f32[1,1024]{1,0:T(1,128)S(1)}, f32[1,1024]{1,0:T(1,128)}, u32[]{:S(2)}) copy-start(f32[1,1024]{1,0:T(1,128)} %get-tuple-element.6) | copy-start | bytes 12292
  510.5 24.3 %copy-start.10 = (f32[1,1024]{1,0:T(1,128)S(1)}, f32[1,1024]{1,0:T(1,128)}, u32[]{:S(2)}) copy-start(f32[1,1024]{1,0:T(1,128)} %get-tuple-element.7) | copy-start | bytes 12292
  510.5 24.3 %copy-start.11 = (f32[1,1024]{1,0:T(1,128)S(1)}, f32[1,1024]{1,0:T(1,128)}, u32[]{:S(2)}) copy-start(f32[1,1024]{1,0:T(1,128)} %get-tuple-element.8) | copy-start | bytes 12292
  564.4 13.4 %copy-start.6 = (bf16[4096,16]{0,1:T(8,128)(2,1)S(1)}, bf16[4096,16]{0,1:T(8,128)(2,1)}, u32[]{:S(2)}) copy-start(bf16[4096,16]{0,1:T(8,128)(2,1)} %param.23) | copy-start | bytes 393220
  564.4 13.4 %copy-start.15 = (f32[16]{0:T(128)S(1)}, f32[16]{0:T(128)}, u32[]{:S(2)}) copy-start(f32[16]{0:T(128)} %param.30) | copy-start | bytes 196
  577.8 14.9 %copy-start.24 = (f32[16]{0:T(128)S(1)}, f32[16]{0:T(128)}, u32[]{:S(2)}) copy-start(f32[16]{0:T(128)} %exponential_negate_fusion) | copy-start | bytes 196
  597.6 8.3 %copy-start.20 = (f32[128]{0:T(128)S(1)}, f32[128]{0:T(128)}, u32[]{:S(2)}) copy-start(f32[128]{0:T(128)} %get-tuple-element.13) | copy-start | bytes 1540
  597.7 8.3 %copy-start.21 = (f32[128]{0:T(128)S(1)}, f32[128]{0:T(128)}, u32[]{:S(2)}) copy-start(f32[128]{0:T(128)} %get-tuple-element.14) | copy-start | bytes 1540
  597.7 8.3 %copy-start.22 = (f32[128]{0:T(128)S(1)}, f32[128]{0:T(128)}, u32[]{:S(2)}) copy-start(f32[128]{0:T(128)} %get-tuple-element.15) | copy-start | bytes 1540
  597.7 8.3 %copy-start.23 = (f32[128]{0:T(128)S(1)}, f32[128]{0:T(128)}, u32[]{:S(2)}) copy-start(f32[128]{0:T(128)} %get-tuple-element.16) | copy-start | bytes 1540
  597.7 9.0 %copy-start.25 = (bf16[4096,128]{1,0:T(8,128)(2,1)S(1)}, bf16[4096,128]{1,0:T(8,128)(2,1)}, u32[]{:S(2)}) copy-start(bf16[4096,128]{1,0:T(8,128)(2,1)} %param.21) | copy-start | bytes 3145732
  606.0 12.3 %slice-start = ((s8[8388608]{0:T(1024)(128)(4,1)}), s8[4194304]{0:T(1024)(128)(4,1)S(1)}, s32[]{:S(2)}) async-start(s8[8388608]{0:T(1024)(128)(4,1)} %bitcast.80), calls=%async_computation.3 | async-start | bytes 8388608
  606.6 8.6 %copy-start.16 = (f32[128]{0:T(128)S(1)}, f32[128]{0:T(128)}, u32[]{:S(2)}) copy-start(f32[128]{0:T(128)} %get-tuple-element.9) | copy-start | bytes 1540
  606.7 8.6 %copy-start.17 = (f32[128]{0:T(128)S(1)}, f32[128]{0:T(128)}, u32[]{:S(2)}) copy-start(f32[128]{0:T(128)} %get-tuple-element.10) | copy-start | bytes 1540
  606.7 8.6 %copy-start.18 = (f32[128]{0:T(128)S(1)}, f32[128]{0:T(128)}, u32[]{:S(2)}) copy-start(f32[128]{0:T(128)} %get-tuple-element.11) | copy-start | bytes 1540
  606.7 8.6 %copy-start.19 = (f32[128]{0:T(128)S(1)}, f32[128]{0:T(128)}, u32[]{:S(2)}) copy-start(f32[128]{0:T(128)} %get-tuple-element.12) | copy-start | bytes 1540
  606.7 11.6 %slice-start.1 = ((s8[8388608]{0:T(1024)(128)(4,1)}), s8[4194304]{0:T(1024)(128)(4,1)S(1)}, s32[]{:S(2)}) async-start(s8[8388608]{0:T(1024)(128)(4,1)} %bitcast.80), calls=%async_computation.4 | async-start | bytes 8388608
  606.7 11.6 %copy-start.12 = (pred[128,128]{1,0:T(8,128)(4,1)S(1)}, pred[128,128]{1,0:T(8,128)(4,1)}, u32[]{:S(2)}) copy-start(pred[128,128]{1,0:T(8,128)(4,1)} %fusion.55) | copy-start | bytes 49156
  606.7 11.6 %copy-start.27 = (f32[16]{0:T(128)S(1)}, f32[16]{0:T(128)}, u32[]{:S(2)}) copy-start(f32[16]{0:T(128)} %param.31) | copy-start | bytes 196
Sparse Core Ops, SparseCore 0:
  9.6 53.4 all-gather.2
  104.7 54.4 all-gather.4
